TPU v7x, 512 devices: a whole 4x8x8 slice. The times are simulated.
512 devices in a mesh: col: 128 (over x, z, y_hi), rep: 4 (over y_lo, core).
Axes of the slice: x: 4, y: 8 (y_hi: 4, y_lo: 2; y = y_hi * 2 + y_lo), z: 8, core: 2. Of those that a mesh axis runs over, the one named last changes fastest.
Arguments:
- tokens: bfloat16 [327680, 768], P(('col', 'rep')), may hold values from -6 to 6
- lengths: int32 [1024], P(('col', 'rep')), may hold values from 1 to 512, as said below
- partner: int32 [1024], P(('col', 'rep')), may hold values from 0 to 1023, as said below
- w_query: bfloat16 [768, 384], replicated, may hold values from -1 to 1
- w_keyval: bfloat16 [768, 768], replicated, may hold values from -1 to 1
- w_output: bfloat16 [384, 768], replicated, may hold values from -0.3125 to 0.3125
Outputs:
- col_loss: float32 [1024], P(('col', 'rep'))
- keyval_grad: float32 [768, 768], P('rep')
Inputs may be any that keep to these rules, and one draw needn't show every extreme that they name: In each block of 2 columns the lengths sum to at most 640; some block sums to exactly 640, and some column has exactly 512 tokens. Columns come in pairs: partner of partner of a column is the column itself, and no column is its own partner.
All inputs are finite; a program needn't handle non-finite values.
Results may differ from a plain program's by a relative error of at most 0.015.
Values may be sent and summed in bfloat16 or wider, within the bound.
A program may use at most 64 MiB of HBM per device.

v0:
```python
import jax
import jax.numpy as jnp
from jax import lax
from jax.sharding import PartitionSpec as P

HEAD = 64


sharpness_divisor = 0.07


def project(tokens, w_keyval):
    return jnp.dot(tokens, w_keyval, preferred_element_type=jnp.float32).astype(jnp.bfloat16)


def attend(keyval, tokens, lengths, w_query, w_output):
    rows = tokens.shape[0]
    count = lengths.shape[0]
    width = w_query.shape[1]
    heads = width // HEAD
    starts = jnp.cumsum(lengths, dtype=jnp.int32) - lengths
    place = jnp.arange(rows, dtype=jnp.int32)
    member = (place[None, :] >= starts[:, None]) & (place[None, :] < (starts + lengths)[:, None])
    first_rows = jnp.take(tokens, starts, axis=0)
    query = jnp.dot(first_rows, w_query, preferred_element_type=jnp.float32).astype(jnp.bfloat16)
    query = query.reshape(count, heads, HEAD)
    keys = keyval[:, :width].reshape(rows, heads, HEAD)
    values = keyval[:, width:].reshape(rows, heads, HEAD)
    scores = jnp.einsum(
        "chd,thd->cht", query.astype(jnp.float32), keys.astype(jnp.float32)
    ) * HEAD ** (-0.5)
    scores = jnp.where(member[:, None, :], scores, -1e30)
    peak = jnp.max(scores, axis=2, keepdims=True)
    lifted = jnp.exp(scores - peak)
    weights = (lifted / jnp.sum(lifted, axis=2, keepdims=True)).astype(jnp.bfloat16)
    mixed = jnp.einsum("cht,thd->chd", weights.astype(jnp.float32), values.astype(jnp.float32))
    mixed = mixed.reshape(count, width).astype(jnp.bfloat16)
    return first_rows.astype(jnp.float32) + jnp.dot(
        mixed, w_output, preferred_element_type=jnp.float32
    )


def similar(left, right):
    return (
        lax.dot_general(left, right, (((1,), (1,)), ((), ())), preferred_element_type=jnp.float32)
        / sharpness_divisor
    )


def gradient_terms(paired_normalized_directions, piece, partner, lse, all_lse):
    cosine_score_matrix = similar(paired_normalized_directions, piece)
    normalized_exponential_shares = jnp.exp(cosine_score_matrix - lse[:, None]).astype(jnp.bfloat16)
    column_logits = similar(piece, paired_normalized_directions)
    column_probs = jnp.exp(column_logits - all_lse[:, None]).astype(jnp.bfloat16)
    index = jnp.arange(piece.shape[0], dtype=jnp.int32)
    match = (index[None, :] == partner[:, None]).astype(jnp.bfloat16)
    rowwise = jnp.dot(normalized_exponential_shares, piece, preferred_element_type=jnp.float32)
    colwise = lax.dot_general(
        column_probs, piece, (((0,), (0,)), ((), ())), preferred_element_type=jnp.float32
    )
    paired_field_encodings = jnp.dot(match, piece, preferred_element_type=jnp.float32)
    return rowwise + colwise - 2.0 * paired_field_encodings


def per_device(tokens, lengths, partner, w_query, w_keyval, w_output):
    keyval = project(tokens, w_keyval)
    embed = attend(keyval, tokens, lengths, w_query, w_output)
    norm = jnp.sqrt(jnp.sum(embed * embed, axis=1, keepdims=True) + 1e-06)
    unit = embed / norm
    paired_normalized_directions = unit.astype(jnp.bfloat16)
    gathered = lax.all_gather(paired_normalized_directions, ("col", "rep"), axis=0, tiled=True)
    cosine_score_matrix = similar(paired_normalized_directions, gathered)
    lse = jnp.log(jnp.sum(jnp.exp(cosine_score_matrix), axis=1))
    index = jnp.arange(gathered.shape[0], dtype=jnp.int32)
    positive = jnp.sum(
        jnp.where(index[None, :] == partner[:, None], cosine_score_matrix, 0.0), axis=1
    )
    col_loss = lse - positive
    all_lse = lax.all_gather(lse, ("col", "rep"), axis=0, tiled=True)
    field_token_total = gradient_terms(
        paired_normalized_directions, gathered, partner, lse, all_lse
    )
    normalized_direction_derivative = field_token_total / sharpness_divisor
    radial = jnp.sum(unit * normalized_direction_derivative, axis=1, keepdims=True)
    dembed = (normalized_direction_derivative - unit * radial) / norm
    _, pull = jax.vjp(lambda inner: attend(inner, tokens, lengths, w_query, w_output), keyval)
    dkeyval = pull(dembed)[0]
    grad_local = lax.dot_general(
        tokens, dkeyval, (((0,), (0,)), ((), ())), preferred_element_type=jnp.float32
    )
    summed_grad = lax.psum(grad_local, ("col", "rep"))
    slab = grad_local.shape[0] // lax.axis_size("rep")
    keyval_grad = lax.dynamic_slice_in_dim(summed_grad, lax.axis_index("rep") * slab, slab, 0)
    return (col_loss, keyval_grad)


def solution(mesh):
    in_specs = (P(("col", "rep"), None), P(("col", "rep")), P(("col", "rep")), P(), P(), P())
    out_specs = (P(("col", "rep")), P("rep", None))
    return jax.shard_map(
        per_device, mesh=mesh, in_specs=in_specs, out_specs=out_specs, check_vma=False
    )
```

profile of v0, /device:TPU:6, one launch (start us, length us, event | category | flops | bytes accessed | tf_op | source)
XLA Modules:
  0.0 526.3 jit_solution(1525650377753924703)
XLA Ops:
  7.2 0.9 reduce-window.8
  8.1 0.7 compare_and_fusion.2
  8.9 1.9 gather_fusion
  10.8 1.3 convolution_convert_fusion.6
  12.2 2.2 convolution_convert_fusion
  15.0 0.3 fusion.33
  15.4 0.3 fusion.6
  15.8 0.3 multiply_reduce_fusion.1
  16.2 0.7 convert_bitcast_fusion
  17.0 118.9 %all-gather.3.cloned.1.call-done = bf16[512,2,768]{2,1,0:T(2,128)(2,1)} async-done(((bf16[1,2,768]{2,1,0:T(2,128)(2,1)}), bf16[512,2,768]{2,1,0:T(2,128)(2,1)}) %all-gather.3.cloned.1.call-update) | async-done | bytes 1572880 | tf_op jit(solution)/shard_map/all_gather | solution.py:71
  135.9 3.7 reshape.138
  139.6 0.3 convolution_multiply_fusion.3
  140.0 0.6 exponential_reduce_fusion
  140.6 0.6 log_dynamic-update-slice_fusion
  141.2 95.3 %all-reduce.2 = f32[1024]{0:T(1024)S(1)} all-reduce(f32[1024]{0:T(1024)S(1)} %get-tuple-element.21), channel_id=1, replica_groups=mesh['col'=128,'rep'=4] {'col','rep'}, use_global_device_ids=true, to_apply=%add.2 | all-reduce | flops 1024 | bytes 8192
  236.5 0.4 fusion.37
  236.9 1.0 multiply_reduce_fusion
  237.8 1.4 convolution_convert_fusion.5
  239.3 0.4 convolution_convert_fusion.1
  240.2 0.4 convolution_convert_fusion.2
  240.6 2.5 convolution_bitcast_fusion
  243.2 273.7 %all-reduce.5.cloned.1.call-done = f32[768,768]{0,1:T(8,128)} async-done(((f32[768,768]{0,1:T(8,128)}), f32[768,768]{0,1:T(8,128)}) %all-reduce.5.cloned.1.call-update) | async-done | bytes 2359312 | tf_op jit(solution)/shard_map/psum | solution.py:91
  516.8 1.5 constant_dynamic-slice_fusion
  518.3 1.1 copy.30
  (31 shorter events, 1.9 us)
Async XLA Ops:
  7.2 5.0 copy-start
  7.2 128.7 %all-gather.3.cloned.1.call-start = ((), (), s32[]{:S(2)}) async-start(), calls=%async_computation.1 | async-start | bytes 1575936 | tf_op jit(solution)/shard_map/all_gather | solution.py:71
  14.4 1.4 copy-start.3
  16.9 499.9 %all-reduce.5.cloned.1.call-start = ((), (), s32[]{:S(2)}) async-start(), calls=%async_computation | async-start | bytes 4718592 | tf_op jit(solution)/shard_map/psum | solution.py:91
  17.0 122.6 %copy-start.1 = (s32[2]{0:T(128)S(1)}, s32[2]{0:T(128)}, u32[]{:S(2)}) copy-start(s32[2]{0:T(128)} %param.10) | copy-start | bytes 28
  237.8 2.8 copy-start.2
Sparse Core Ops, SparseCore 0:
  17.0 118.8 all-gather.2
  243.3 273.4 all-reduce.4
where the time goes:
time: 529 us; the launch traced here: 526 us
  waiting for transfers between devices  393 us (74%)
  blocking collectives  95.3 us (18%)
  between operations  14.2 us (3%)
  matrix products  11.6 us (2%)
  local copies, waits for them, and re-layouts  9.11 us (2%)
    psum x1, waiting for transfers between devices, per_device(): summed_grad = lax.psum(grad_local, ('col', 'rep'))  274 us
    all_gather x1, waiting for transfers between devices, per_device(): lax.all_gather(paired_normalized_directions, ('col', 'rep'), axis=0, tile...  119 us
    unnamed x1, blocking collectives  95.3 us
  transfers between devices with their start and end apart: 2, of which 2 were waited for; matrix products, arithmetic and copies ran while one was open for 0% of the time, Pallas kernels for 0%

commit v1 on v0

v1 whole, which is shorter than its diff:
```python
import functools

import jax
import jax.numpy as jnp
from jax import lax
from jax.experimental import pallas as pl
from jax.experimental.pallas import tpu as pltpu
from jax.sharding import PartitionSpec as P

HEAD = 64
SHARP = 0.07
BF = jnp.bfloat16
F32 = jnp.float32
MESH = pl.DeviceIdType.MESH
NX, NY, NZ = 4, 8, 8
NEAR = (1, 7, 2, 6, 3, 5, 4)

XC = [(dx, dk) for dx in range(NX) for dk in range(2) if (dx, dk) != (0, 0)]
XY = [(dx, dh) for dx in range(NX) for dh in range(4) if (dx, dh) != (0, 0)]
PEERS = sorted(
    {(dx, 0, 0, dk) for dx, dk in XC}
    | {(0, j, 0, 0) for j in NEAR}
    | {(0, 0, j, 0) for j in NEAR}
    | {(dx, 2 * dh, 0, 0) for dx, dh in XY}
)


def mm(a, b):
    return jnp.dot(a, b, preferred_element_type=F32)


def mm_t(a, b):
    return lax.dot_general(a, b, (((1,), (1,)), ((), ())), preferred_element_type=F32)


def mm_tl(a, b):
    return lax.dot_general(a, b, (((0,), (0,)), ((), ())), preferred_element_type=F32)


def two(a):
    high = a.astype(BF)
    low = (a - high.astype(F32)).astype(BF)
    return jnp.concatenate([high, low], axis=0)


def fold(a):
    return a[:16] + a[16:]


def device(x, y, z, k):
    return ((x * NZ + z) * 4 + y // 2, lax.rem(y, 2) * 2 + k)


def kernel(
    lens, part, tok, wq, wkv, wo,
    loss_out, grad_out,
    a1_s, a1_r, u, tperm, early_s, early_r, late_s, late_r, r2_s, r2_r, r3_r, ag_r,
    soft, a1_ss, a1_rs, a2_ss, a2_rs, a3_ss, a3_rs, fw_ss, fw_rs,
    e_ss, e_rs, l_ss, l_rs, r2_ss, r2_rs, r3_ss, r3_rs, ag_ss, ag_rs,
):
    col, rep = lax.axis_index("col"), lax.axis_index("rep")
    x, z = col // 32, lax.rem(col // 4, 8)
    yh, yl, k = lax.rem(col, 4), rep // 2, lax.rem(rep, 2)
    y = yh * 2 + yl
    m = x * 2 + k

    def at(dx, dy, dz, dk):
        return (
            lax.rem(x + dx, NX), lax.rem(y + dy, NY), lax.rem(z + dz, NZ), lax.rem(k + dk, 2)
        )

    def remote(src, dst, ss, rs, place):
        return pltpu.make_async_remote_copy(
            src_ref=src, dst_ref=dst, send_sem=ss, recv_sem=rs,
            device_id=device(*place), device_id_type=MESH,
        )

    barrier = pltpu.get_barrier_semaphore()
    for off in PEERS:
        pl.semaphore_signal(
            barrier, inc=1, device_id=device(*at(*off)), device_id_type=MESH
        )

    row = lax.broadcasted_iota(jnp.int32, (16, 640), 0)
    pos = lax.broadcasted_iota(jnp.int32, (16, 640), 1)
    l0, l1 = lens[0], lens[1]
    lo = jnp.where(row < 8, 0, l0)
    hi = jnp.where(row < 8, l0, l0 + l1)
    t = tok[...]
    first = mm((pos == lo).astype(F32).astype(BF), t)
    hrow = lax.rem(lax.broadcasted_iota(jnp.int32, (16, 384), 0), 8)
    own_head = lax.broadcasted_iota(jnp.int32, (16, 384), 1) // HEAD == hrow
    query = mm(first.astype(BF), wq[...]).astype(BF).astype(F32)
    qexp = jnp.where(own_head, query, 0.0).astype(BF)
    wk, wv = wkv[:, :384], wkv[:, 384:]
    scores = fold(mm_t(two(mm_t(qexp, wk)), t)) * HEAD ** (-0.5)
    scores = jnp.where((pos >= lo) & (pos < hi), scores, -1e30)
    lifted = jnp.exp(scores - jnp.max(scores, axis=1, keepdims=True))
    weights = lifted / jnp.sum(lifted, axis=1, keepdims=True)
    soft[...] = weights
    wb = weights.astype(BF)
    pooled = mm(wb, t)
    mixed = jnp.where(own_head, fold(mm(two(pooled), wv)), 0.0)
    mixed = jnp.sum(mixed.reshape(2, 8, 384), axis=1, keepdims=True)
    mixed = jnp.broadcast_to(mixed, (2, 8, 384)).reshape(16, 384).astype(BF)
    embed = first + mm(mixed, wo[...])
    norm = jnp.sqrt(jnp.sum(embed * embed, axis=1, keepdims=True) + 1e-06)
    unit = embed / norm
    unit_b = unit.astype(BF)
    ub = unit_b.astype(F32)
    row16 = lax.broadcasted_iota(jnp.int32, (16, 768), 0)
    placed = jnp.where(row16 == 2 * m, ub[0:1], jnp.where(row16 == 2 * m + 1, ub[8:9], 0.0))
    placed = placed.astype(BF)
    a1_s[0] = placed[:, :384]
    a1_s[1] = placed[:, 384:]

    pl.semaphore_wait(barrier, len(PEERS))

    def group_copies(src, dst, ss, rs):
        copies = []
        for dx, dk in XC:
            place = at(dx, 0, 0, dk)
            slot = dx * 2 + dk
            copies.append(remote(src(place), dst.at[slot], ss.at[slot], rs.at[slot], place))
        return copies

    a1 = group_copies(lambda p: a1_s.at[p[3]], a1_r, a1_ss, a1_rs)
    for cp in a1:
        cp.start()

    lane = lax.broadcasted_iota(jnp.int32, (768, 128), 1)
    deep = lax.broadcasted_iota(jnp.int32, (768, 128), 0)
    py, pv = lane // 16, lax.rem(lane, 16)
    base = lax.rem(py, 2) * 384 + (py // 2) * 12 + pv
    base = jnp.where(pv < 12, base, 100000)

    def permute(i):
        want = base + ((i % 2) * 192 + (i // 2) * 48)
        pick = (deep == want).astype(F32).astype(BF)
        tperm[i] = mm(tok[...], pick).astype(BF)

    for i in range(2):
        permute(i)
    for cp in a1:
        cp.wait_recv()
    block = a1_s[k].astype(F32)
    for s in range(1, 8):
        block = block + a1_r[s].astype(F32)
    block = block.astype(BF)

    def gather(half):
        lanes = slice(half * 384, half * 384 + 384)
        u[z, y, :, lanes] = block
        mine = u.at[z, y, :, lanes]

        def line(j, second):
            along_z = (half == 0) == second
            return at(0, 0, j, 0) if along_z else at(0, j, 0, 0)

        def plane(j):
            p = at(0, 8 - j, 8 - j, 0)
            return u.at[p[2], :, :, lanes] if half == 0 else u.at[:, p[1], :, lanes]

        own = u.at[z, :, :, lanes] if half == 0 else u.at[:, y, :, lanes]
        a2 = [remote(mine, mine, a2_ss.at[j], a2_rs.at[j], line(j, False)) for j in NEAR]
        for cp in a2:
            cp.start()
        for i in range(2, 8):
            permute(i)
        for cp in a2:
            cp.wait_recv()
        a3 = [remote(own, own, a3_ss.at[j], a3_rs.at[j], line(j, True)) for j in NEAR]
        for cp in a3:
            cp.start()
        fw = []
        for n, j in enumerate((0,) + NEAR):
            if n:
                a3[n - 1].wait_recv()
            reg = own if j == 0 else plane(j)
            cp = remote(reg, reg, fw_ss.at[j], fw_rs.at[j], at(0, 0, 0, 1))
            cp.start()
            fw.append(cp)
            if n == 0:
                for i in range(8):
                    early_s[i, :, 0:128] = mm(wb, tperm[i]).astype(BF)
                    early_s[i, :, 128:512] = qexp
                e = group_copies(lambda p: early_s.at[p[0] * 2 + p[3]], early_r, e_ss, e_rs)
                for cp in e:
                    cp.start()
        for cp in fw:
            cp.wait_recv()
        for cp in a2 + a3 + fw:
            cp.wait_send()
        for cp in e:
            cp.wait()

    pl.when(k == 0)(functools.partial(gather, 0))
    pl.when(k == 1)(functools.partial(gather, 1))
    for cp in a1:
        cp.wait_send()

    scale = 1.0 / SHARP
    total = jnp.zeros((1, 1024), F32)
    whole = u[...].reshape(1024, 768)
    for i in range(4):
        part_s = mm_t(u[2 * i : 2 * i + 2].reshape(256, 768), whole)
        total = total + jnp.sum(jnp.exp(part_s * scale), axis=0, keepdims=True)
    all_lse = jnp.log(total)
    logits = mm_t(unit_b, whole) * scale
    lse = jnp.log(jnp.sum(jnp.exp(logits), axis=1, keepdims=True))
    n = lax.broadcasted_iota(jnp.int32, (16, 1024), 1)
    nz, ny, nm, nc = n // 128, lax.rem(n // 16, 8), lax.rem(n // 2, 8), lax.rem(n, 2)
    number = (((nm // 2) * 8 + nz) * 4 + ny // 2) * 4 + lax.rem(ny, 2) * 2 + lax.rem(nm, 2)
    number = number * 2 + nc
    lrow = lax.broadcasted_iota(jnp.int32, (16, 1024), 0)
    match = number == jnp.where(lrow < 8, part[0], part[1])
    positive = jnp.sum(jnp.where(match, logits, 0.0), axis=1, keepdims=True)
    loss_out[...] = jnp.broadcast_to(lse - positive, (16, 128))
    rowp = jnp.exp(logits - lse).astype(BF)
    colp = jnp.exp(logits - all_lse).astype(BF)
    stack = jnp.concatenate([rowp, colp, match.astype(F32).astype(BF)], axis=0)
    terms = mm(stack, whole)
    dunit = (terms[:16] + terms[16:32] - 2.0 * terms[32:]) / SHARP
    radial = jnp.sum(unit * dunit, axis=1, keepdims=True)
    dembed = (dunit - unit * radial) / norm

    dmixed = fold(mm_t(two(dembed), wo[...])).astype(BF).astype(F32)
    dmexp = jnp.where(own_head, dmixed, 0.0).astype(BF)
    dweights = fold(mm_t(two(mm_t(dmexp, wv)), t)).astype(BF).astype(F32)
    weights = soft[...]
    dscores = weights * (dweights - jnp.sum(weights * dweights, axis=1, keepdims=True))
    ds2 = two(dscores * HEAD ** (-0.5))
    for i in range(8):
        late_s[i, :, 0:128] = fold(mm(ds2, tperm[i])).astype(BF)
        late_s[i, :, 128:512] = dmexp
    late = group_copies(lambda p: late_s.at[p[0] * 2 + p[3]], late_r, l_ss, l_rs)
    for cp in late:
        cp.start()
    early_r[0] = early_s[m]
    late_r[0] = late_s[m]
    for cp in late:
        cp.wait_recv()

    keys = mm_tl(late_r[:, :, 0:128].reshape(128, 128), early_r[:, :, 128:512].reshape(128, 384))
    vals = mm_tl(early_r[:, :, 0:128].reshape(128, 128), late_r[:, :, 128:512].reshape(128, 384))
    r2_s[:, :, 0:384] = keys.astype(BF).reshape(8, 16, 384)
    r2_s[:, :, 384:768] = vals.astype(BF).reshape(8, 16, 384)
    r2 = []
    for j in NEAR:
        place = at(0, j, 0, 0)
        cp = remote(r2_s.at[place[1]], r2_r.at[j], r2_ss.at[j], r2_rs.at[j], place)
        cp.start()
        r2.append(cp)
    sum2 = r2_s[y].astype(F32)
    for cp, j in zip(r2, NEAR):
        cp.wait_recv()
        sum2 = sum2 + r2_r[j].astype(F32)
    r3_r[z] = sum2.astype(BF)
    r3 = []
    for j in NEAR:
        cp = remote(r3_r.at[z], r3_r.at[z], r3_ss.at[j], r3_rs.at[j], at(0, 0, j, 0))
        cp.start()
        r3.append(cp)
    for cp in r3:
        cp.wait_recv()
    sum3 = r3_r[0].astype(F32)
    for j in range(1, 8):
        sum3 = sum3 + r3_r[j].astype(F32)
    mine = x * 4 + yh
    ag_r[mine] = sum3.astype(BF)
    ag = []
    for dx, dh in XY:
        cp = remote(
            ag_r.at[mine], ag_r.at[mine], ag_ss.at[dx * 4 + dh], ag_rs.at[dx * 4 + dh],
            at(dx, 2 * dh, 0, 0),
        )
        cp.start()
        ag.append(cp)
    for cp in ag:
        cp.wait_recv()
    for i in range(16):
        grad_out[12 * i : 12 * i + 12, :] = ag_r[i].astype(F32)[0:12]
    for cp in late + r2 + r3 + ag:
        cp.wait_send()


def per_device(tokens, lengths, partner, w_query, w_keyval, w_output):
    smem = pl.BlockSpec(memory_space=pltpu.SMEM)
    vmem = pl.BlockSpec(memory_space=pltpu.VMEM)
    dma = pltpu.SemaphoreType.DMA
    loss, grad = pl.pallas_call(
        kernel,
        name="contrast",
        out_shape=(
            jax.ShapeDtypeStruct((16, 128), F32),
            jax.ShapeDtypeStruct((192, 768), F32),
        ),
        in_specs=[smem, smem, vmem, vmem, vmem, vmem],
        out_specs=(vmem, vmem),
        scratch_shapes=[
            pltpu.VMEM((2, 16, 384), BF),
            pltpu.VMEM((8, 16, 384), BF),
            pltpu.VMEM((8, 8, 16, 768), BF),
            pltpu.VMEM((8, 640, 128), BF),
            pltpu.VMEM((8, 16, 512), BF),
            pltpu.VMEM((8, 16, 512), BF),
            pltpu.VMEM((8, 16, 512), BF),
            pltpu.VMEM((8, 16, 512), BF),
            pltpu.VMEM((8, 16, 768), BF),
            pltpu.VMEM((8, 16, 768), BF),
            pltpu.VMEM((8, 16, 768), BF),
            pltpu.VMEM((16, 16, 768), BF),
            pltpu.VMEM((16, 640), F32),
        ]
        + [dma((8,))] * 16
        + [dma((16,))] * 2,
        compiler_params=pltpu.CompilerParams(
            collective_id=0, has_side_effects=True, vmem_limit_bytes=48 * 2**20
        ),
    )(lengths, partner, tokens, w_query, w_keyval, w_output)
    return loss[::8, 0], grad


def solution(mesh):
    in_specs = (P(("col", "rep"), None), P(("col", "rep")), P(("col", "rep")), P(), P(), P())
    out_specs = (P(("col", "rep")), P("rep", None))
    return jax.shard_map(
        per_device, mesh=mesh, in_specs=in_specs, out_specs=out_specs, check_vma=False
    )
```

time: 529 us -> 80.3 us (0.15)
  waiting for transfers between devices: 393 us -> 0 us
  blocking collectives: 95.3 us -> 0 us
  Pallas kernels: 0 us -> 71.6 us
  between operations: 14.2 us -> 0.65 us
  matrix products: 11.6 us -> 0 us
    psum x1 -> x0, waiting for transfers between devices: 274 us -> none  [per_device(): summed_grad = lax.psum(grad_local, ('col', 'rep'))]
    all_gather x1 -> x0, waiting for transfers between devices: 119 us -> none  [per_device(): lax.all_gather(paired_normalized_directions, ('col', 'rep'), axis=0, tile...]
    unnamed x1 -> x0, blocking collectives: 95.3 us -> none
    pallas_call x0 -> x1, Pallas kernels: none -> 71.6 us  [per_device(): pl.pallas_call(kernel, name='contrast', out_shape=(jax.ShapeDtypeStruct((...]
    dot_general x14 -> x0, matrix products: 11.6 us -> none  [the longest x1 2.5 us: per_device(): lax.dot_general(tokens, dkeyval, (((0,), (0,)), ((), ())), preferred_elem...]
  transfers between devices with their start and end apart: 2 -> 0, of which waited for: 2 -> 0; matrix products, arithmetic and copies ran while one was open for 0% -> 0% of each run, Pallas kernels for 0% -> 0%
where the time goes in v1:
time: 80.3 us; the launch traced here: 79.7 us
  Pallas kernels  71.6 us (89%)
  local copies, waits for them, and re-layouts  6.74 us (8%)
    pallas_call x1, Pallas kernels, per_device(): pl.pallas_call(kernel, name='contrast', out_shape=(jax.ShapeDtypeStruct((...  71.6 us
    unnamed x13, local copies, waits for them, and re-layouts  6.72 us

profile of v1, /device:TPU:6, one launch (start us, length us, event | category | flops | bytes accessed | tf_op | source)
XLA Modules:
  0.0 79.7 jit_solution(15746053604818358378)
XLA Ops:
  0.6 0.0 copy-start
  0.6 1.3 %copy-done = bf16[768,768]{1,0:T(8,128)(2,1)S(1)} copy-done((bf16[768,768]{1,0:T(8,128)(2,1)S(1)}, bf16[768,768]{1,0:T(8,128)(2,1)}, u32[]{:S(2)}) %copy-start) | copy-done | bytes 1179672
  1.9 0.0 copy-start.1
  1.9 1.2 %copy-done.1 = bf16[640,768]{1,0:T(8,128)(2,1)S(1)} copy-done((bf16[640,768]{1,0:T(8,128)(2,1)S(1)}, bf16[640,768]{1,0:T(8,128)(2,1)}, u32[]{:S(2)}) %copy-start.1) | copy-done | bytes 983064
  3.1 0.0 copy-start.2
  3.1 1.1 %copy-done.2 = bf16[768,384]{1,0:T(8,128)(2,1)S(1)} copy-done((bf16[768,384]{1,0:T(8,128)(2,1)S(1)}, bf16[768,384]{1,0:T(8,128)(2,1)}, u32[]{:S(2)}) %copy-start.2) | copy-done | bytes 589848
  4.2 0.0 copy-start.3
  4.2 1.1 %copy-done.3 = bf16[384,768]{1,0:T(8,128)(2,1)S(1)} copy-done((bf16[384,768]{1,0:T(8,128)(2,1)S(1)}, bf16[384,768]{1,0:T(8,128)(2,1)}, u32[]{:S(2)}) %copy-start.3) | copy-done | bytes 589848
  5.2 0.0 copy-start.4
  5.2 0.7 copy-done.4
  5.9 0.0 copy-start.5
  5.9 0.7 copy-done.5
  6.5 71.6 %contrast.1 = (f32[16,128]{1,0:T(8,128)S(1)}, f32[192,768]{1,0:T(8,128)S(1)}) custom-call(s32[2]{0:T(128)S(1)} %copy-done.4, s32[2]{0:T(128)S(1)} %copy-done.5, bf16[640,768]{1,0:T(8,128)(2,1)S(1)} %copy-done.1, bf16[768,384]{1,0:T(8,128)(2,1)S(1)} %copy-done.2, bf16[768,768]{1,0:T(8,128)(2,1)S(1)} %copy-done, bf16[384,768]{1,0:T(8,128)(2,1)S(1)} %copy-done.3), custom_call_target="tpu_custom_call" | custom-call | tf_op jit(solution)/shard_map/contrast/pallas_call | solution.py:291
  78.2 0.6 reduce
  78.9 0.8 %copy.9 = f32[192,768]{1,0:T(8,128)} copy(f32[192,768]{1,0:T(8,128)S(1)} %get-tuple-element.9) | data formatting | bytes 1179648
  (1 shorter events, 0.0 us)
Async XLA Ops:
  0.6 1.3 %copy-start = (bf16[768,768]{1,0:T(8,128)(2,1)S(1)}, bf16[768,768]{1,0:T(8,128)(2,1)}, u32[]{:S(2)}) copy-start(bf16[768,768]{1,0:T(8,128)(2,1)} %wkv.1) | copy-start | bytes 3538948
  1.9 1.2 %copy-start.1 = (bf16[640,768]{1,0:T(8,128)(2,1)S(1)}, bf16[640,768]{1,0:T(8,128)(2,1)}, u32[]{:S(2)}) copy-start(bf16[640,768]{1,0:T(8,128)(2,1)} %tok.1) | copy-start | bytes 2949124
  3.1 1.1 %copy-start.2 = (bf16[768,384]{1,0:T(8,128)(2,1)S(1)}, bf16[768,384]{1,0:T(8,128)(2,1)}, u32[]{:S(2)}) copy-start(bf16[768,384]{1,0:T(8,128)(2,1)} %wq.1) | copy-start | bytes 1769476
  4.2 1.1 %copy-start.3 = (bf16[384,768]{1,0:T(8,128)(2,1)S(1)}, bf16[384,768]{1,0:T(8,128)(2,1)}, u32[]{:S(2)}) copy-start(bf16[384,768]{1,0:T(8,128)(2,1)} %wo.1) | copy-start | bytes 1769476
  5.2 0.7 copy-start.4
  5.9 0.7 copy-start.5

commit v2 on v1

--- a/solution.py
+++ b/solution.py
@@ -16,12 +16,12 @@
 NEAR = (1, 7, 2, 6, 3, 5, 4)
 
 XC = [(dx, dk) for dx in range(NX) for dk in range(2) if (dx, dk) != (0, 0)]
-XY = [(dx, dh) for dx in range(NX) for dh in range(4) if (dx, dh) != (0, 0)]
+XZ = [(dx, dz) for dx in range(NX) for dz in (0,) + NEAR if (dx, dz) != (0, 0)]
 PEERS = sorted(
     {(dx, 0, 0, dk) for dx, dk in XC}
     | {(0, j, 0, 0) for j in NEAR}
     | {(0, 0, j, 0) for j in NEAR}
-    | {(dx, 2 * dh, 0, 0) for dx, dh in XY}
+    | {(dx, 0, dz, 0) for dx, dz in XZ}
 )
 
 
@@ -52,9 +52,10 @@
 
 
 def kernel(
-    lens, part, tok, wq, wkv, wo,
+    lens_h, part_h, tok_h, wq_h, wkv_h, wo_h,
     loss_out, grad_out,
-    a1_s, a1_r, u, tperm, early_s, early_r, late_s, late_r, r2_s, r2_r, r3_r, ag_r,
+    lens, part, tok, wq, wkv, wo, in_s,
+    a1_s, a1_r, u, tperm, early_s, early_r, late_s, late_r, r2_s, r2_r, r3_s, r3_r, ag_r,
     soft, a1_ss, a1_rs, a2_ss, a2_rs, a3_ss, a3_rs, fw_ss, fw_rs,
     e_ss, e_rs, l_ss, l_rs, r2_ss, r2_rs, r3_ss, r3_rs, ag_ss, ag_rs,
 ):
@@ -75,6 +76,14 @@
             device_id=device(*place), device_id_type=MESH,
         )
 
+    loads = [
+        pltpu.make_async_copy(src, dst, in_s.at[i])
+        for i, (src, dst) in enumerate(
+            [(lens_h, lens), (tok_h, tok), (wq_h, wq), (wkv_h, wkv), (wo_h, wo), (part_h, part)]
+        )
+    ]
+    for cp in loads:
+        cp.start()
     barrier = pltpu.get_barrier_semaphore()
     for off in PEERS:
         pl.semaphore_signal(
@@ -83,6 +92,8 @@
 
     row = lax.broadcasted_iota(jnp.int32, (16, 640), 0)
     pos = lax.broadcasted_iota(jnp.int32, (16, 640), 1)
+    loads[0].wait()
+    loads[1].wait()
     l0, l1 = lens[0], lens[1]
     lo = jnp.where(row < 8, 0, l0)
     hi = jnp.where(row < 8, l0, l0 + l1)
@@ -90,8 +101,10 @@
     first = mm((pos == lo).astype(F32).astype(BF), t)
     hrow = lax.rem(lax.broadcasted_iota(jnp.int32, (16, 384), 0), 8)
     own_head = lax.broadcasted_iota(jnp.int32, (16, 384), 1) // HEAD == hrow
+    loads[2].wait()
     query = mm(first.astype(BF), wq[...]).astype(BF).astype(F32)
     qexp = jnp.where(own_head, query, 0.0).astype(BF)
+    loads[3].wait()
     wk, wv = wkv[:, :384], wkv[:, 384:]
     scores = fold(mm_t(two(mm_t(qexp, wk)), t)) * HEAD ** (-0.5)
     scores = jnp.where((pos >= lo) & (pos < hi), scores, -1e30)
@@ -103,6 +116,7 @@
     mixed = jnp.where(own_head, fold(mm(two(pooled), wv)), 0.0)
     mixed = jnp.sum(mixed.reshape(2, 8, 384), axis=1, keepdims=True)
     mixed = jnp.broadcast_to(mixed, (2, 8, 384)).reshape(16, 384).astype(BF)
+    loads[4].wait()
     embed = first + mm(mixed, wo[...])
     norm = jnp.sqrt(jnp.sum(embed * embed, axis=1, keepdims=True) + 1e-06)
     unit = embed / norm
@@ -128,19 +142,14 @@
     for cp in a1:
         cp.start()
 
-    lane = lax.broadcasted_iota(jnp.int32, (768, 128), 1)
-    deep = lax.broadcasted_iota(jnp.int32, (768, 128), 0)
-    py, pv = lane // 16, lax.rem(lane, 16)
-    base = lax.rem(py, 2) * 384 + (py // 2) * 12 + pv
-    base = jnp.where(pv < 12, base, 100000)
-
     def permute(i):
-        want = base + ((i % 2) * 192 + (i // 2) * 48)
-        pick = (deep == want).astype(F32).astype(BF)
+        lane = lax.broadcasted_iota(jnp.int32, (768, 128), 1)
+        deep = lax.broadcasted_iota(jnp.int32, (768, 128), 0)
+        pz, pl_, pv = lane // 16, lax.rem(lane // 8, 2), lax.rem(lane, 8)
+        want = pl_ * 384 + pz * 6 + pv + ((i % 2) * 192 + (i // 2) * 48)
+        pick = ((deep == want) & (pv < 6)).astype(F32).astype(BF)
         tperm[i] = mm(tok[...], pick).astype(BF)
 
-    for i in range(2):
-        permute(i)
     for cp in a1:
         cp.wait_recv()
     block = a1_s[k].astype(F32)
@@ -165,8 +174,6 @@
         a2 = [remote(mine, mine, a2_ss.at[j], a2_rs.at[j], line(j, False)) for j in NEAR]
         for cp in a2:
             cp.start()
-        for i in range(2, 8):
-            permute(i)
         for cp in a2:
             cp.wait_recv()
         a3 = [remote(own, own, a3_ss.at[j], a3_rs.at[j], line(j, True)) for j in NEAR]
@@ -182,6 +189,7 @@
             fw.append(cp)
             if n == 0:
                 for i in range(8):
+                    permute(i)
                     early_s[i, :, 0:128] = mm(wb, tperm[i]).astype(BF)
                     early_s[i, :, 128:512] = qexp
                 e = group_copies(lambda p: early_s.at[p[0] * 2 + p[3]], early_r, e_ss, e_rs)
@@ -213,6 +221,7 @@
     number = (((nm // 2) * 8 + nz) * 4 + ny // 2) * 4 + lax.rem(ny, 2) * 2 + lax.rem(nm, 2)
     number = number * 2 + nc
     lrow = lax.broadcasted_iota(jnp.int32, (16, 1024), 0)
+    loads[5].wait()
     match = number == jnp.where(lrow < 8, part[0], part[1])
     positive = jnp.sum(jnp.where(match, logits, 0.0), axis=1, keepdims=True)
     loss_out[...] = jnp.broadcast_to(lse - positive, (16, 128))
@@ -247,45 +256,52 @@
     r2_s[:, :, 384:768] = vals.astype(BF).reshape(8, 16, 384)
     r2 = []
     for j in NEAR:
-        place = at(0, j, 0, 0)
-        cp = remote(r2_s.at[place[1]], r2_r.at[j], r2_ss.at[j], r2_rs.at[j], place)
+        place = at(0, 0, j, 0)
+        cp = remote(r2_s.at[place[2]], r2_r.at[j], r2_ss.at[j], r2_rs.at[j], place)
         cp.start()
         r2.append(cp)
-    sum2 = r2_s[y].astype(F32)
+    sum2 = r2_s[z].astype(F32)
     for cp, j in zip(r2, NEAR):
         cp.wait_recv()
         sum2 = sum2 + r2_r[j].astype(F32)
-    r3_r[z] = sum2.astype(BF)
+    for i in range(2):
+        half = sum2[8 * i : 8 * i + 8]
+        r3_s[i] = jnp.concatenate([half[:, :384], half[:, 384:]], axis=0).astype(BF)
     r3 = []
     for j in NEAR:
-        cp = remote(r3_r.at[z], r3_r.at[z], r3_ss.at[j], r3_rs.at[j], at(0, 0, j, 0))
+        place = at(0, j, 0, 0)
+        src = r3_s.at[lax.rem(place[1], 2)]
+        cp = remote(src, r3_r.at[y], r3_ss.at[j], r3_rs.at[j], place)
         cp.start()
         r3.append(cp)
+    r3_r[y] = r3_s[yl]
     for cp in r3:
         cp.wait_recv()
     sum3 = r3_r[0].astype(F32)
     for j in range(1, 8):
         sum3 = sum3 + r3_r[j].astype(F32)
-    mine = x * 4 + yh
+    mine = x * 8 + z
     ag_r[mine] = sum3.astype(BF)
     ag = []
-    for dx, dh in XY:
+    for dx, dz in XZ:
         cp = remote(
-            ag_r.at[mine], ag_r.at[mine], ag_ss.at[dx * 4 + dh], ag_rs.at[dx * 4 + dh],
-            at(dx, 2 * dh, 0, 0),
+            ag_r.at[mine], ag_r.at[mine], ag_ss.at[dx * 8 + dz], ag_rs.at[dx * 8 + dz],
+            at(dx, 0, dz, 0),
         )
         cp.start()
         ag.append(cp)
+    orow = lax.broadcasted_iota(jnp.int32, (192, 512), 0)
+    want = lax.broadcasted_iota(jnp.int32, (192, 512), 1) - ((orow // 6) * 16 + lax.rem(orow, 6))
     for cp in ag:
         cp.wait_recv()
-    for i in range(16):
-        grad_out[12 * i : 12 * i + 12, :] = ag_r[i].astype(F32)[0:12]
+    pieces = ag_r[...].reshape(512, 384)
+    grad_out[:, :384] = mm((want == 0).astype(F32).astype(BF), pieces)
+    grad_out[:, 384:] = mm((want == 8).astype(F32).astype(BF), pieces)
     for cp in late + r2 + r3 + ag:
         cp.wait_send()
 
 
 def per_device(tokens, lengths, partner, w_query, w_keyval, w_output):
-    smem = pl.BlockSpec(memory_space=pltpu.SMEM)
     vmem = pl.BlockSpec(memory_space=pltpu.VMEM)
     dma = pltpu.SemaphoreType.DMA
     loss, grad = pl.pallas_call(
@@ -295,9 +311,16 @@
             jax.ShapeDtypeStruct((16, 128), F32),
             jax.ShapeDtypeStruct((192, 768), F32),
         ),
-        in_specs=[smem, smem, vmem, vmem, vmem, vmem],
+        in_specs=[pl.BlockSpec(memory_space=pl.ANY)] * 6,
         out_specs=(vmem, vmem),
         scratch_shapes=[
+            pltpu.SMEM((2,), jnp.int32),
+            pltpu.SMEM((2,), jnp.int32),
+            pltpu.VMEM((640, 768), BF),
+            pltpu.VMEM((768, 384), BF),
+            pltpu.VMEM((768, 768), BF),
+            pltpu.VMEM((384, 768), BF),
+            dma((6,)),
             pltpu.VMEM((2, 16, 384), BF),
             pltpu.VMEM((8, 16, 384), BF),
             pltpu.VMEM((8, 8, 16, 768), BF),
@@ -308,14 +331,15 @@
             pltpu.VMEM((8, 16, 512), BF),
             pltpu.VMEM((8, 16, 768), BF),
             pltpu.VMEM((8, 16, 768), BF),
-            pltpu.VMEM((8, 16, 768), BF),
-            pltpu.VMEM((16, 16, 768), BF),
+            pltpu.VMEM((2, 16, 384), BF),
+            pltpu.VMEM((8, 16, 384), BF),
+            pltpu.VMEM((32, 16, 384), BF),
             pltpu.VMEM((16, 640), F32),
         ]
         + [dma((8,))] * 16
-        + [dma((16,))] * 2,
+        + [dma((32,))] * 2,
         compiler_params=pltpu.CompilerParams(
-            collective_id=0, has_side_effects=True, vmem_limit_bytes=48 * 2**20
+            collective_id=0, has_side_effects=True, vmem_limit_bytes=60 * 2**20
         ),
     )(lengths, partner, tokens, w_query, w_keyval, w_output)
     return loss[::8, 0], grad

time: 80.3 us -> 76.1 us (0.948)
  local copies, waits for them, and re-layouts: 6.74 us -> 2.63 us
    unnamed x13 -> x1, local copies, waits for them, and re-layouts: 6.72 us -> 1.92 us
where the time goes in v2:
time: 76.1 us; the launch traced here: 75.4 us
  Pallas kernels  71.5 us (94%)
  local copies, waits for them, and re-layouts  2.63 us (3%)
    pallas_call x1, Pallas kernels, per_device(): pl.pallas_call(kernel, name='contrast', out_shape=(jax.ShapeDtypeStruct((...  71.5 us
    unnamed x1, local copies, waits for them, and re-layouts  1.92 us

profile of v2, /device:TPU:6, one launch (start us, length us, event | category | flops | bytes accessed | tf_op | source)
XLA Modules:
  0.0 75.4 jit_solution(6879004087918395341)
XLA Ops:
  0.6 71.5 %contrast.1 = (f32[16,128]{1,0:T(8,128)}, f32[192,768]{1,0:T(8,128)}) custom-call(s32[2]{0:T(128)} %lens_h.1, s32[2]{0:T(128)} %part_h.1, bf16[640,768]{1,0:T(8,128)(2,1)} %tok_h.1, bf16[768,384]{1,0:T(8,128)(2,1)} %wq_h.1, bf16[768,768]{1,0:T(8,128)(2,1)} %wkv_h.1, bf16[384,768]{1,0:T(8,128)(2,1)} %wo_h.1), custom_call_target="tpu_custom_call" | custom-call | tf_op jit(solution)/shard_map/contrast/pallas_call | solution.py:307
  72.1 0.7 slice.3
  72.8 0.6 reduce
  73.5 1.9 %copy.9 = f32[192,768]{1,0:T(8,128)} copy(f32[192,768]{1,0:T(8,128)} %get-tuple-element.9) | data formatting | bytes 1179648

commit v3 on v2

--- a/solution.py
+++ b/solution.py
@@ -17,11 +17,13 @@
 
 XC = [(dx, dk) for dx in range(NX) for dk in range(2) if (dx, dk) != (0, 0)]
 XZ = [(dx, dz) for dx in range(NX) for dz in (0,) + NEAR if (dx, dz) != (0, 0)]
+XY = [(dx, dh) for dx in range(NX) for dh in (0, 1, 3, 2) if (dx, dh) != (0, 0)]
 PEERS = sorted(
     {(dx, 0, 0, dk) for dx, dk in XC}
     | {(0, j, 0, 0) for j in NEAR}
     | {(0, 0, j, 0) for j in NEAR}
     | {(dx, 0, dz, 0) for dx, dz in XZ}
+    | {(dx, 2 * dh, 0, 0) for dx, dh in XY}
 )
 
 
@@ -55,9 +57,11 @@
     lens_h, part_h, tok_h, wq_h, wkv_h, wo_h,
     loss_out, grad_out,
     lens, part, tok, wq, wkv, wo, in_s,
-    a1_s, a1_r, u, tperm, early_s, early_r, late_s, late_r, r2_s, r2_r, r3_s, r3_r, ag_r,
+    a1_s, a1_r, u, tperm, early_s, early_r, late_s, late_r, r2k_s, r2k_r, r2v_s, r2v_r,
+    r3k_s, r3k_r, r3v_r, agk_r, agv_r,
     soft, a1_ss, a1_rs, a2_ss, a2_rs, a3_ss, a3_rs, fw_ss, fw_rs,
-    e_ss, e_rs, l_ss, l_rs, r2_ss, r2_rs, r3_ss, r3_rs, ag_ss, ag_rs,
+    e_ss, e_rs, l_ss, l_rs, r2k_ss, r2k_rs, r2v_ss, r2v_rs,
+    r3k_ss, r3k_rs, r3v_ss, r3v_rs, agv_ss, agv_rs, agk_ss, agk_rs,
 ):
     col, rep = lax.axis_index("col"), lax.axis_index("rep")
     x, z = col // 32, lax.rem(col // 4, 8)
@@ -113,6 +117,7 @@
     soft[...] = weights
     wb = weights.astype(BF)
     pooled = mm(wb, t)
+    pooled_b = pooled.astype(BF)
     mixed = jnp.where(own_head, fold(mm(two(pooled), wv)), 0.0)
     mixed = jnp.sum(mixed.reshape(2, 8, 384), axis=1, keepdims=True)
     mixed = jnp.broadcast_to(mixed, (2, 8, 384)).reshape(16, 384).astype(BF)
@@ -142,13 +147,17 @@
     for cp in a1:
         cp.start()
 
+    lane = lax.broadcasted_iota(jnp.int32, (768, 128), 1)
+    deep = lax.broadcasted_iota(jnp.int32, (768, 128), 0)
+    part8, pos16, pos8 = lane // 16, lax.rem(lane, 16), lax.rem(lane, 8)
+    by_z = jnp.where(pos8 < 6, (pos16 // 8) * 384 + part8 * 6 + pos8, 100000)
+    by_y = jnp.where(pos16 < 12, lax.rem(part8, 2) * 384 + (part8 // 2) * 12 + pos16, 100000)
+
+    def pick(base, i):
+        return (deep == base + ((i % 2) * 192 + (i // 2) * 48)).astype(F32).astype(BF)
+
     def permute(i):
-        lane = lax.broadcasted_iota(jnp.int32, (768, 128), 1)
-        deep = lax.broadcasted_iota(jnp.int32, (768, 128), 0)
-        pz, pl_, pv = lane // 16, lax.rem(lane // 8, 2), lax.rem(lane, 8)
-        want = pl_ * 384 + pz * 6 + pv + ((i % 2) * 192 + (i // 2) * 48)
-        pick = ((deep == want) & (pv < 6)).astype(F32).astype(BF)
-        tperm[i] = mm(tok[...], pick).astype(BF)
+        tperm[i] = mm(tok[...], pick(by_z, i)).astype(BF)
 
     for cp in a1:
         cp.wait_recv()
@@ -174,6 +183,8 @@
         a2 = [remote(mine, mine, a2_ss.at[j], a2_rs.at[j], line(j, False)) for j in NEAR]
         for cp in a2:
             cp.start()
+        for i in range(3):
+            permute(i)
         for cp in a2:
             cp.wait_recv()
         a3 = [remote(own, own, a3_ss.at[j], a3_rs.at[j], line(j, True)) for j in NEAR]
@@ -188,9 +199,10 @@
             cp.start()
             fw.append(cp)
             if n == 0:
+                for i in range(3, 8):
+                    permute(i)
                 for i in range(8):
-                    permute(i)
-                    early_s[i, :, 0:128] = mm(wb, tperm[i]).astype(BF)
+                    early_s[i, :, 0:128] = mm(pooled_b, pick(by_y, i)).astype(BF)
                     early_s[i, :, 128:512] = qexp
                 e = group_copies(lambda p: early_s.at[p[0] * 2 + p[3]], early_r, e_ss, e_rs)
                 for cp in e:
@@ -251,53 +263,89 @@
         cp.wait_recv()
 
     keys = mm_tl(late_r[:, :, 0:128].reshape(128, 128), early_r[:, :, 128:512].reshape(128, 384))
-    vals = mm_tl(early_r[:, :, 0:128].reshape(128, 128), late_r[:, :, 128:512].reshape(128, 384))
-    r2_s[:, :, 0:384] = keys.astype(BF).reshape(8, 16, 384)
-    r2_s[:, :, 384:768] = vals.astype(BF).reshape(8, 16, 384)
-    r2 = []
+    r2k_s[...] = keys.astype(BF).reshape(8, 16, 384)
+    r2k, r2v = [], []
     for j in NEAR:
         place = at(0, 0, j, 0)
-        cp = remote(r2_s.at[place[2]], r2_r.at[j], r2_ss.at[j], r2_rs.at[j], place)
-        cp.start()
-        r2.append(cp)
-    sum2 = r2_s[z].astype(F32)
-    for cp, j in zip(r2, NEAR):
-        cp.wait_recv()
-        sum2 = sum2 + r2_r[j].astype(F32)
+        cp = remote(r2k_s.at[place[2]], r2k_r.at[j], r2k_ss.at[j], r2k_rs.at[j], place)
+        cp.start()
+        r2k.append(cp)
+    vals = mm_tl(early_r[:, :, 0:128].reshape(128, 128), late_r[:, :, 128:512].reshape(128, 384))
+    r2v_s[...] = vals.astype(BF).reshape(8, 16, 384)
+    for j in NEAR:
+        place = at(0, j, 0, 0)
+        cp = remote(r2v_s.at[place[1]], r2v_r.at[j], r2v_ss.at[j], r2v_rs.at[j], place)
+        cp.start()
+        r2v.append(cp)
+
+    sum2 = r2k_s[z].astype(F32)
+    for cp, j in zip(r2k, NEAR):
+        cp.wait_recv()
+        sum2 = sum2 + r2k_r[j].astype(F32)
     for i in range(2):
         half = sum2[8 * i : 8 * i + 8]
-        r3_s[i] = jnp.concatenate([half[:, :384], half[:, 384:]], axis=0).astype(BF)
-    r3 = []
+        tiles = [half[:, :128], half[:, 128:256], half[:, 256:], jnp.zeros((8, 128), F32)]
+        r3k_s[i] = jnp.concatenate(tiles, axis=0).astype(BF)
+    r3k, r3v = [], []
     for j in NEAR:
         place = at(0, j, 0, 0)
-        src = r3_s.at[lax.rem(place[1], 2)]
-        cp = remote(src, r3_r.at[y], r3_ss.at[j], r3_rs.at[j], place)
-        cp.start()
-        r3.append(cp)
-    r3_r[y] = r3_s[yl]
-    for cp in r3:
-        cp.wait_recv()
-    sum3 = r3_r[0].astype(F32)
+        src = r3k_s.at[lax.rem(place[1], 2)]
+        cp = remote(src, r3k_r.at[y], r3k_ss.at[j], r3k_rs.at[j], place)
+        cp.start()
+        r3k.append(cp)
+    r3k_r[y] = r3k_s[yl]
+    sum2 = r2v_s[y].astype(F32)
+    for cp, j in zip(r2v, NEAR):
+        cp.wait_recv()
+        sum2 = sum2 + r2v_r[j].astype(F32)
+    r3v_r[z] = sum2.astype(BF)
+    for j in NEAR:
+        cp = remote(r3v_r.at[z], r3v_r.at[z], r3v_ss.at[j], r3v_rs.at[j], at(0, 0, j, 0))
+        cp.start()
+        r3v.append(cp)
+
+    for cp in r3k:
+        cp.wait_recv()
+    sum3 = r3k_r[0].astype(F32)
     for j in range(1, 8):
-        sum3 = sum3 + r3_r[j].astype(F32)
+        sum3 = sum3 + r3k_r[j].astype(F32)
     mine = x * 8 + z
-    ag_r[mine] = sum3.astype(BF)
+    agk_r[mine] = sum3.astype(BF)
     ag = []
     for dx, dz in XZ:
-        cp = remote(
-            ag_r.at[mine], ag_r.at[mine], ag_ss.at[dx * 8 + dz], ag_rs.at[dx * 8 + dz],
-            at(dx, 0, dz, 0),
-        )
+        slot = dx * 8 + dz
+        own = agk_r.at[mine]
+        cp = remote(own, own, agk_ss.at[slot], agk_rs.at[slot], at(dx, 0, dz, 0))
         cp.start()
         ag.append(cp)
-    orow = lax.broadcasted_iota(jnp.int32, (192, 512), 0)
-    want = lax.broadcasted_iota(jnp.int32, (192, 512), 1) - ((orow // 6) * 16 + lax.rem(orow, 6))
+    for cp in r3v:
+        cp.wait_recv()
+    sum3 = r3v_r[0].astype(F32)
+    for j in range(1, 8):
+        sum3 = sum3 + r3v_r[j].astype(F32)
+    mine_v = x * 4 + yh
+    agv_r[mine_v] = sum3.astype(BF)
+    for dx, dh in XY:
+        slot = dx * 4 + dh
+        own = agv_r.at[mine_v]
+        cp = remote(own, own, agv_ss.at[slot], agv_rs.at[slot], at(dx, 2 * dh, 0, 0))
+        cp.start()
+        ag.append(cp)
+    krow = lax.broadcasted_iota(jnp.int32, (192, 1024), 0)
+    kpos = lax.broadcasted_iota(jnp.int32, (192, 1024), 1)
+    kpos = kpos - ((krow // 6) * 32 + lax.rem(krow, 6))
+    vrow = lax.broadcasted_iota(jnp.int32, (192, 256), 0)
+    vpos = lax.broadcasted_iota(jnp.int32, (192, 256), 1)
+    vpos = vpos - ((vrow // 12) * 16 + lax.rem(vrow, 12))
+    ksel = [(kpos == 8 * c).astype(F32).astype(BF) for c in range(3)]
+    vsel = (vpos == 0).astype(F32).astype(BF)
     for cp in ag:
         cp.wait_recv()
-    pieces = ag_r[...].reshape(512, 384)
-    grad_out[:, :384] = mm((want == 0).astype(F32).astype(BF), pieces)
-    grad_out[:, 384:] = mm((want == 8).astype(F32).astype(BF), pieces)
-    for cp in late + r2 + r3 + ag:
+    pieces = agk_r[...].reshape(1024, 128)
+    for c in range(3):
+        grad_out[:, 128 * c : 128 * c + 128] = mm(ksel[c], pieces)
+    grad_out[:, 384:] = mm(vsel, agv_r[...].reshape(256, 384))
+    for cp in late + r2k + r2v + r3k + r3v + ag:
         cp.wait_send()
 
 
@@ -329,14 +377,19 @@
             pltpu.VMEM((8, 16, 512), BF),
             pltpu.VMEM((8, 16, 512), BF),
             pltpu.VMEM((8, 16, 512), BF),
-            pltpu.VMEM((8, 16, 768), BF),
-            pltpu.VMEM((8, 16, 768), BF),
-            pltpu.VMEM((2, 16, 384), BF),
-            pltpu.VMEM((8, 16, 384), BF),
-            pltpu.VMEM((32, 16, 384), BF),
+            pltpu.VMEM((8, 16, 384), BF),
+            pltpu.VMEM((8, 16, 384), BF),
+            pltpu.VMEM((8, 16, 384), BF),
+            pltpu.VMEM((8, 16, 384), BF),
+            pltpu.VMEM((2, 32, 128), BF),
+            pltpu.VMEM((8, 32, 128), BF),
+            pltpu.VMEM((8, 16, 384), BF),
+            pltpu.VMEM((32, 32, 128), BF),
+            pltpu.VMEM((16, 16, 384), BF),
             pltpu.VMEM((16, 640), F32),
         ]
-        + [dma((8,))] * 16
+        + [dma((8,))] * 20
+        + [dma((16,))] * 2
         + [dma((32,))] * 2,
         compiler_params=pltpu.CompilerParams(
             collective_id=0, has_side_effects=True, vmem_limit_bytes=60 * 2**20

time: 76.1 us -> 74.3 us (0.976)
  Pallas kernels: 71.5 us -> 69.6 us
    pallas_call x1, Pallas kernels: 71.5 us -> 69.6 us  [per_device(): pl.pallas_call(kernel, name='contrast', out_shape=(jax.ShapeDtypeStruct((...]
where the time goes in v3:
time: 74.3 us; the launch traced here: 73.5 us
  Pallas kernels  69.6 us (94%)
  local copies, waits for them, and re-layouts  2.63 us (4%)
    pallas_call x1, Pallas kernels, per_device(): pl.pallas_call(kernel, name='contrast', out_shape=(jax.ShapeDtypeStruct((...  69.6 us
    unnamed x1, local copies, waits for them, and re-layouts  1.92 us

profile of v3, /device:TPU:6, one launch (start us, length us, event | category | flops | bytes accessed | tf_op | source)
XLA Modules:
  0.0 73.5 jit_solution(13541890209175856411)
XLA Ops:
  0.6 69.6 %contrast.1 = (f32[16,128]{1,0:T(8,128)}, f32[192,768]{1,0:T(8,128)}) custom-call(s32[2]{0:T(128)} %lens_h.1, s32[2]{0:T(128)} %part_h.1, bf16[640,768]{1,0:T(8,128)(2,1)} %tok_h.1, bf16[768,384]{1,0:T(8,128)(2,1)} %wq_h.1, bf16[768,768]{1,0:T(8,128)(2,1)} %wkv_h.1, bf16[384,768]{1,0:T(8,128)(2,1)} %wo_h.1), custom_call_target="tpu_custom_call" | custom-call | tf_op jit(solution)/shard_map/contrast/pallas_call | solution.py:355
  70.3 0.7 slice.3
  71.0 0.6 reduce
  71.6 1.9 %copy.9 = f32[192,768]{1,0:T(8,128)} copy(f32[192,768]{1,0:T(8,128)} %get-tuple-element.9) | data formatting | bytes 1179648

commit v4 on v3

--- a/solution.py
+++ b/solution.py
@@ -13,11 +13,25 @@
 F32 = jnp.float32
 MESH = pl.DeviceIdType.MESH
 NX, NY, NZ = 4, 8, 8
-NEAR = (1, 7, 2, 6, 3, 5, 4)
-
-XC = [(dx, dk) for dx in range(NX) for dk in range(2) if (dx, dk) != (0, 0)]
-XZ = [(dx, dz) for dx in range(NX) for dz in (0,) + NEAR if (dx, dz) != (0, 0)]
-XY = [(dx, dh) for dx in range(NX) for dh in (0, 1, 3, 2) if (dx, dh) != (0, 0)]
+NEAR = (4, 3, 5, 2, 6, 1, 7)
+
+
+def hops(offset):
+    return -sum(min(d, size - d) for d, size in offset)
+
+
+XC = sorted(
+    [(dx, dk) for dx in range(NX) for dk in range(2) if (dx, dk) != (0, 0)],
+    key=lambda o: hops([(o[0], NX)]),
+)
+XZ = sorted(
+    [(dx, dz) for dx in range(NX) for dz in range(NZ) if (dx, dz) != (0, 0)],
+    key=lambda o: hops([(o[0], NX), (o[1], NZ)]),
+)
+XY = sorted(
+    [(dx, dh) for dx in range(NX) for dh in range(4) if (dx, dh) != (0, 0)],
+    key=lambda o: hops([(o[0], NX), (2 * o[1], NY)]),
+)
 PEERS = sorted(
     {(dx, 0, 0, dk) for dx, dk in XC}
     | {(0, j, 0, 0) for j in NEAR}
@@ -236,7 +250,9 @@
     loads[5].wait()
     match = number == jnp.where(lrow < 8, part[0], part[1])
     positive = jnp.sum(jnp.where(match, logits, 0.0), axis=1, keepdims=True)
-    loss_out[...] = jnp.broadcast_to(lse - positive, (16, 128))
+    loss = lse - positive
+    loss_lane = lax.broadcasted_iota(jnp.int32, (8, 128), 1)
+    loss_out[...] = jnp.where(loss_lane == 0, loss[0:8], loss[8:16])
     rowp = jnp.exp(logits - lse).astype(BF)
     colp = jnp.exp(logits - all_lse).astype(BF)
     stack = jnp.concatenate([rowp, colp, match.astype(F32).astype(BF)], axis=0)
@@ -343,8 +359,8 @@
         cp.wait_recv()
     pieces = agk_r[...].reshape(1024, 128)
     for c in range(3):
-        grad_out[:, 128 * c : 128 * c + 128] = mm(ksel[c], pieces)
-    grad_out[:, 384:] = mm(vsel, agv_r[...].reshape(256, 384))
+        grad_out[:, 128 * c : 128 * c + 128] = mm(ksel[c], pieces).astype(BF)
+    grad_out[:, 384:] = mm(vsel, agv_r[...].reshape(256, 384)).astype(BF)
     for cp in late + r2k + r2v + r3k + r3v + ag:
         cp.wait_send()
 
@@ -356,8 +372,8 @@
         kernel,
         name="contrast",
         out_shape=(
-            jax.ShapeDtypeStruct((16, 128), F32),
-            jax.ShapeDtypeStruct((192, 768), F32),
+            jax.ShapeDtypeStruct((8, 128), F32),
+            jax.ShapeDtypeStruct((192, 768), BF),
         ),
         in_specs=[pl.BlockSpec(memory_space=pl.ANY)] * 6,
         out_specs=(vmem, vmem),
@@ -395,7 +411,7 @@
             collective_id=0, has_side_effects=True, vmem_limit_bytes=60 * 2**20
         ),
     )(lengths, partner, tokens, w_query, w_keyval, w_output)
-    return loss[::8, 0], grad
+    return loss[0, :2], grad.astype(F32)
 
 
 def solution(mesh):

time: 74.3 us -> 69.8 us (0.939)
  Pallas kernels: 69.6 us -> 66 us
  local copies, waits for them, and re-layouts: 2.63 us -> 1.19 us
  other arithmetic: 0.63 us -> 1.81 us
    pallas_call x1, Pallas kernels: 69.6 us -> 66 us  [per_device(): pl.pallas_call(kernel, name='contrast', out_shape=(jax.ShapeDtypeStruct((...]
    unnamed x1 -> x0, local copies, waits for them, and re-layouts: 1.92 us -> none
    convert_element_type x0 -> x1, other arithmetic: none -> 1.81 us  [per_device(): return (loss[0, :2], grad.astype(F32))]
    squeeze x0 -> x1, local copies, waits for them, and re-layouts: none -> 1.19 us  [per_device(): return (loss[0, :2], grad.astype(F32))]
where the time goes in v4:
time: 69.8 us; the launch traced here: 69.7 us
  Pallas kernels  66 us (95%)
  other arithmetic  1.81 us (3%)
  local copies, waits for them, and re-layouts  1.19 us (2%)
    pallas_call x1, Pallas kernels, per_device(): pl.pallas_call(kernel, name='contrast', out_shape=(jax.ShapeDtypeStruct((...  66 us
    convert_element_type x1, other arithmetic, per_device(): return (loss[0, :2], grad.astype(F32))  1.81 us

profile of v4, /device:TPU:6, one launch (start us, length us, event | category | flops | bytes accessed | tf_op | source)
XLA Modules:
  0.0 69.7 jit_solution(8838578902688876136)
XLA Ops:
  0.6 66.0 %contrast.1 = (f32[8,128]{1,0:T(8,128)}, bf16[192,768]{1,0:T(8,128)(2,1)}) custom-call(s32[2]{0:T(128)} %lens_h.1, s32[2]{0:T(128)} %part_h.1, bf16[640,768]{1,0:T(8,128)(2,1)} %tok_h.1, bf16[768,384]{1,0:T(8,128)(2,1)} %wq_h.1, bf16[768,768]{1,0:T(8,128)(2,1)} %wkv_h.1, bf16[384,768]{1,0:T(8,128)(2,1)} %wo_h.1), custom_call_target="tpu_custom_call" | custom-call | tf_op jit(solution)/shard_map/contrast/pallas_call | solution.py:371
  66.6 1.2 %slice_bitcast_fusion = f32[2]{0:T(128)} fusion(f32[8,128]{1,0:T(8,128)} %get-tuple-element.4), kind=kLoop, calls=%fused_computation | loop fusion | bytes 16 | tf_op jit(solution)/shard_map/squeeze | solution.py:414
  67.8 1.8 %convert_element_type.3 = f32[192,768]{1,0:T(8,128)} convert(bf16[192,768]{1,0:T(8,128)(2,1)} %get-tuple-element.5) | non-fusion elementwise | flops 147456 | bytes 884736 | tf_op jit(solution)/shard_map/convert_element_type | solution.py:414

commit v5 on v4

--- a/solution.py
+++ b/solution.py
@@ -68,13 +68,13 @@
 
 
 def kernel(
-    lens_h, part_h, tok_h, wq_h, wkv_h, wo_h,
+    meta_h, tok_h, wq_h, wkv_h, wo_h,
     loss_out, grad_out,
-    lens, part, tok, wq, wkv, wo, in_s,
-    a1_s, a1_r, u, tperm, early_s, early_r, late_s, late_r, r2k_s, r2k_r, r2v_s, r2v_r,
+    meta, tok, wq, wkv, wo, in_s,
+    a1_s, a1_r, u, tperm, early_s, early_r, late_s, late_r, dm_s, dm_r, r2k_s, r2k_r, r2v_s, r2v_r,
     r3k_s, r3k_r, r3v_r, agk_r, agv_r,
     soft, a1_ss, a1_rs, a2_ss, a2_rs, a3_ss, a3_rs, fw_ss, fw_rs,
-    e_ss, e_rs, l_ss, l_rs, r2k_ss, r2k_rs, r2v_ss, r2v_rs,
+    e_ss, e_rs, l_ss, l_rs, d_ss, d_rs, r2k_ss, r2k_rs, r2v_ss, r2v_rs,
     r3k_ss, r3k_rs, r3v_ss, r3v_rs, agv_ss, agv_rs, agk_ss, agk_rs,
 ):
     col, rep = lax.axis_index("col"), lax.axis_index("rep")
@@ -97,7 +97,7 @@
     loads = [
         pltpu.make_async_copy(src, dst, in_s.at[i])
         for i, (src, dst) in enumerate(
-            [(lens_h, lens), (tok_h, tok), (wq_h, wq), (wkv_h, wkv), (wo_h, wo), (part_h, part)]
+            [(meta_h, meta), (tok_h, tok), (wq_h, wq), (wkv_h, wkv), (wo_h, wo)]
         )
     ]
     for cp in loads:
@@ -112,7 +112,7 @@
     pos = lax.broadcasted_iota(jnp.int32, (16, 640), 1)
     loads[0].wait()
     loads[1].wait()
-    l0, l1 = lens[0], lens[1]
+    l0, l1 = meta[0], meta[1]
     lo = jnp.where(row < 8, 0, l0)
     hi = jnp.where(row < 8, l0, l0 + l1)
     t = tok[...]
@@ -173,6 +173,8 @@
     def permute(i):
         tperm[i] = mm(tok[...], pick(by_z, i)).astype(BF)
 
+    for i in range(2):
+        permute(i)
     for cp in a1:
         cp.wait_recv()
     block = a1_s[k].astype(F32)
@@ -194,16 +196,21 @@
             return u.at[p[2], :, :, lanes] if half == 0 else u.at[:, p[1], :, lanes]
 
         own = u.at[z, :, :, lanes] if half == 0 else u.at[:, y, :, lanes]
-        a2 = [remote(mine, mine, a2_ss.at[j], a2_rs.at[j], line(j, False)) for j in NEAR]
-        for cp in a2:
-            cp.start()
-        for i in range(3):
-            permute(i)
-        for cp in a2:
-            cp.wait_recv()
+        a2 = {j: remote(mine, mine, a2_ss.at[j], a2_rs.at[j], line(j, False)) for j in NEAR}
+        for j in NEAR:
+            a2[j].start()
+
+        def spread(j):
+            p = at(0, 8 - j, 8 - j, 0)
+            part = u.at[z, p[1], :, lanes] if half == 0 else u.at[p[2], y, :, lanes]
+            for d in NEAR:
+                remote(part, part, a3_ss.at[d], a3_rs.at[d], line(d, True)).start()
+
+        spread(8)
+        for j in reversed(NEAR):
+            a2[j].wait_recv()
+            spread(j)
         a3 = [remote(own, own, a3_ss.at[j], a3_rs.at[j], line(j, True)) for j in NEAR]
-        for cp in a3:
-            cp.start()
         fw = []
         for n, j in enumerate((0,) + NEAR):
             if n:
@@ -213,7 +220,7 @@
             cp.start()
             fw.append(cp)
             if n == 0:
-                for i in range(3, 8):
+                for i in range(2, 8):
                     permute(i)
                 for i in range(8):
                     early_s[i, :, 0:128] = mm(pooled_b, pick(by_y, i)).astype(BF)
@@ -223,7 +230,7 @@
                     cp.start()
         for cp in fw:
             cp.wait_recv()
-        for cp in a2 + a3 + fw:
+        for cp in list(a2.values()) + a3 + fw:
             cp.wait_send()
         for cp in e:
             cp.wait()
@@ -247,8 +254,7 @@
     number = (((nm // 2) * 8 + nz) * 4 + ny // 2) * 4 + lax.rem(ny, 2) * 2 + lax.rem(nm, 2)
     number = number * 2 + nc
     lrow = lax.broadcasted_iota(jnp.int32, (16, 1024), 0)
-    loads[5].wait()
-    match = number == jnp.where(lrow < 8, part[0], part[1])
+    match = number == jnp.where(lrow < 8, meta[2], meta[3])
     positive = jnp.sum(jnp.where(match, logits, 0.0), axis=1, keepdims=True)
     loss = lse - positive
     loss_lane = lax.broadcasted_iota(jnp.int32, (8, 128), 1)
@@ -263,37 +269,42 @@
 
     dmixed = fold(mm_t(two(dembed), wo[...])).astype(BF).astype(F32)
     dmexp = jnp.where(own_head, dmixed, 0.0).astype(BF)
+    dm_s[...] = dmexp
+    dm = group_copies(lambda p: dm_s, dm_r, d_ss, d_rs)
+    for cp in dm:
+        cp.start()
+    dm_r[0] = dmexp
     dweights = fold(mm_t(two(mm_t(dmexp, wv)), t)).astype(BF).astype(F32)
     weights = soft[...]
     dscores = weights * (dweights - jnp.sum(weights * dweights, axis=1, keepdims=True))
     ds2 = two(dscores * HEAD ** (-0.5))
     for i in range(8):
-        late_s[i, :, 0:128] = fold(mm(ds2, tperm[i])).astype(BF)
-        late_s[i, :, 128:512] = dmexp
+        late_s[i] = fold(mm(ds2, tperm[i])).astype(BF)
     late = group_copies(lambda p: late_s.at[p[0] * 2 + p[3]], late_r, l_ss, l_rs)
     for cp in late:
         cp.start()
     early_r[0] = early_s[m]
     late_r[0] = late_s[m]
-    for cp in late:
-        cp.wait_recv()
-
-    keys = mm_tl(late_r[:, :, 0:128].reshape(128, 128), early_r[:, :, 128:512].reshape(128, 384))
-    r2k_s[...] = keys.astype(BF).reshape(8, 16, 384)
+
     r2k, r2v = [], []
-    for j in NEAR:
-        place = at(0, 0, j, 0)
-        cp = remote(r2k_s.at[place[2]], r2k_r.at[j], r2k_ss.at[j], r2k_rs.at[j], place)
-        cp.start()
-        r2k.append(cp)
-    vals = mm_tl(early_r[:, :, 0:128].reshape(128, 128), late_r[:, :, 128:512].reshape(128, 384))
+    for cp in dm:
+        cp.wait_recv()
+    vals = mm_tl(early_r[:, :, 0:128].reshape(128, 128), dm_r[...].reshape(128, 384))
     r2v_s[...] = vals.astype(BF).reshape(8, 16, 384)
     for j in NEAR:
         place = at(0, j, 0, 0)
         cp = remote(r2v_s.at[place[1]], r2v_r.at[j], r2v_ss.at[j], r2v_rs.at[j], place)
         cp.start()
         r2v.append(cp)
-
+    for cp in late:
+        cp.wait_recv()
+    keys = mm_tl(late_r[...].reshape(128, 128), early_r[:, :, 128:512].reshape(128, 384))
+    r2k_s[...] = keys.astype(BF).reshape(8, 16, 384)
+    for j in NEAR:
+        place = at(0, 0, j, 0)
+        cp = remote(r2k_s.at[place[2]], r2k_r.at[j], r2k_ss.at[j], r2k_rs.at[j], place)
+        cp.start()
+        r2k.append(cp)
     sum2 = r2k_s[z].astype(F32)
     for cp, j in zip(r2k, NEAR):
         cp.wait_recv()
@@ -361,7 +372,7 @@
     for c in range(3):
         grad_out[:, 128 * c : 128 * c + 128] = mm(ksel[c], pieces).astype(BF)
     grad_out[:, 384:] = mm(vsel, agv_r[...].reshape(256, 384)).astype(BF)
-    for cp in late + r2k + r2v + r3k + r3v + ag:
+    for cp in dm + late + r2k + r2v + r3k + r3v + ag:
         cp.wait_send()
 
 
@@ -375,24 +386,25 @@
             jax.ShapeDtypeStruct((8, 128), F32),
             jax.ShapeDtypeStruct((192, 768), BF),
         ),
-        in_specs=[pl.BlockSpec(memory_space=pl.ANY)] * 6,
+        in_specs=[pl.BlockSpec(memory_space=pl.ANY)] * 5,
         out_specs=(vmem, vmem),
         scratch_shapes=[
-            pltpu.SMEM((2,), jnp.int32),
-            pltpu.SMEM((2,), jnp.int32),
+            pltpu.SMEM((4,), jnp.int32),
             pltpu.VMEM((640, 768), BF),
             pltpu.VMEM((768, 384), BF),
             pltpu.VMEM((768, 768), BF),
             pltpu.VMEM((384, 768), BF),
-            dma((6,)),
+            dma((5,)),
             pltpu.VMEM((2, 16, 384), BF),
             pltpu.VMEM((8, 16, 384), BF),
             pltpu.VMEM((8, 8, 16, 768), BF),
             pltpu.VMEM((8, 640, 128), BF),
             pltpu.VMEM((8, 16, 512), BF),
             pltpu.VMEM((8, 16, 512), BF),
-            pltpu.VMEM((8, 16, 512), BF),
-            pltpu.VMEM((8, 16, 512), BF),
+            pltpu.VMEM((8, 16, 128), BF),
+            pltpu.VMEM((8, 16, 128), BF),
+            pltpu.VMEM((16, 384), BF),
+            pltpu.VMEM((8, 16, 384), BF),
             pltpu.VMEM((8, 16, 384), BF),
             pltpu.VMEM((8, 16, 384), BF),
             pltpu.VMEM((8, 16, 384), BF),
@@ -404,13 +416,13 @@
             pltpu.VMEM((16, 16, 384), BF),
             pltpu.VMEM((16, 640), F32),
         ]
-        + [dma((8,))] * 20
+        + [dma((8,))] * 22
         + [dma((16,))] * 2
         + [dma((32,))] * 2,
         compiler_params=pltpu.CompilerParams(
-            collective_id=0, has_side_effects=True, vmem_limit_bytes=60 * 2**20
+            collective_id=0, has_side_effects=True, vmem_limit_bytes=107 * 2**19
         ),
-    )(lengths, partner, tokens, w_query, w_keyval, w_output)
+    )(jnp.concatenate([lengths, partner]), tokens, w_query, w_keyval, w_output)
     return loss[0, :2], grad.astype(F32)
 
 

time: 69.8 us -> 67.5 us (0.967)
  Pallas kernels: 66 us -> 64.6 us
    pallas_call x1, Pallas kernels: 66 us -> 64.6 us  [per_device(): pl.pallas_call(kernel, name='contrast', out_shape=(jax.ShapeDtypeStruct((...]
    convert_element_type x1, other arithmetic: 1.81 us -> 0.85 us  [per_device(): return (loss[0, :2], grad.astype(F32))]
    concatenate x0 -> x1, other arithmetic: none -> 0.75 us  [per_device(): jnp.concatenate([lengths, partner])]
where the time goes in v5:
time: 67.5 us; the launch traced here: 67.4 us
  Pallas kernels  64.6 us (96%)
  other arithmetic  1.6 us (2%)
    pallas_call x1, Pallas kernels, per_device(): pl.pallas_call(kernel, name='contrast', out_shape=(jax.ShapeDtypeStruct((...  64.6 us

profile of v5, /device:TPU:6, one launch (start us, length us, event | category | flops | bytes accessed | tf_op | source)
XLA Modules:
  0.0 67.4 jit_solution(12631988424414395665)
XLA Ops:
  0.6 0.7 %pad_add_fusion.meta_h = s32[4]{0:T(128)S(1)} fusion(s32[2]{0:T(128)} %param.8, s32[2]{0:T(128)} %param.7), kind=kLoop, calls=%fused_computation | loop fusion | flops 4 | bytes 32 | tf_op jit(solution)/shard_map/concatenate | solution.py:425
  1.4 64.6 %contrast.1 = (f32[8,128]{1,0:T(8,128)S(1)}, bf16[192,768]{1,0:T(8,128)(2,1)S(1)}) custom-call(s32[4]{0:T(128)S(1)} %pad_add_fusion.meta_h, bf16[640,768]{1,0:T(8,128)(2,1)} %tok_h.1, bf16[768,384]{1,0:T(8,128)(2,1)} %wq_h.1, bf16[768,768]{1,0:T(8,128)(2,1)} %wkv_h.1, bf16[384,768]{1,0:T(8,128)(2,1)} %wo_h.1), custom_call_target="tpu_custom_call" | custom-call | tf_op jit(solution)/shard_map/contrast/pallas_call | solution.py:382
  66.0 0.5 slice_bitcast_fusion
  66.5 0.9 %convert_element_type.3 = f32[192,768]{1,0:T(8,128)} convert(bf16[192,768]{1,0:T(8,128)(2,1)S(1)} %get-tuple-element.5) | non-fusion elementwise | flops 147456 | bytes 884736 | tf_op jit(solution)/shard_map/convert_element_type | solution.py:426

commit v6 on v5

--- a/solution.py
+++ b/solution.py
@@ -210,9 +210,10 @@
         for j in reversed(NEAR):
             a2[j].wait_recv()
             spread(j)
-        a3 = [remote(own, own, a3_ss.at[j], a3_rs.at[j], line(j, True)) for j in NEAR]
+        near = NEAR[::-1]
+        a3 = [remote(own, own, a3_ss.at[j], a3_rs.at[j], line(j, True)) for j in near]
         fw = []
-        for n, j in enumerate((0,) + NEAR):
+        for n, j in enumerate((0,) + near):
             if n:
                 a3[n - 1].wait_recv()
             reg = own if j == 0 else plane(j)
@@ -241,13 +242,23 @@
         cp.wait_send()
 
     scale = 1.0 / SHARP
-    total = jnp.zeros((1, 1024), F32)
     whole = u[...].reshape(1024, 768)
+    totals = [jnp.zeros((1, 256), F32)] * 4
     for i in range(4):
-        part_s = mm_t(u[2 * i : 2 * i + 2].reshape(256, 768), whole)
-        total = total + jnp.sum(jnp.exp(part_s * scale), axis=0, keepdims=True)
-    all_lse = jnp.log(total)
-    logits = mm_t(unit_b, whole) * scale
+        rows = u[2 * i : 2 * i + 2].reshape(256, 768)
+        if i == 0:
+            rows = jnp.concatenate([rows, unit_b], axis=0)
+        block_s = mm_t(rows, u[2 * i :].reshape(1024 - 256 * i, 768)) * scale
+        if i == 0:
+            logits, block_s = block_s[256:], block_s[:256]
+        expd = jnp.exp(block_s)
+        down = jnp.sum(expd, axis=0, keepdims=True)
+        for j in range(i, 4):
+            totals[j] = totals[j] + down[:, 256 * (j - i) : 256 * (j - i) + 256]
+        if i < 3:
+            ones = jnp.ones((16, 768 - 256 * i), BF)
+            totals[i] = totals[i] + mm_t(ones, expd[:, 256:].astype(BF))[0:1]
+    all_lse = jnp.log(jnp.concatenate(totals, axis=1))
     lse = jnp.log(jnp.sum(jnp.exp(logits), axis=1, keepdims=True))
     n = lax.broadcasted_iota(jnp.int32, (16, 1024), 1)
     nz, ny, nm, nc = n // 128, lax.rem(n // 16, 8), lax.rem(n // 2, 8), lax.rem(n, 2)

time: 67.5 us -> 66.5 us (0.985)
  Pallas kernels: 64.6 us -> 63 us
    pallas_call x1, Pallas kernels: 64.6 us -> 63 us  [per_device(): pl.pallas_call(kernel, name='contrast', out_shape=(jax.ShapeDtypeStruct((...]
where the time goes in v6:
time: 66.5 us; the launch traced here: 65.8 us
  Pallas kernels  63 us (95%)
  other arithmetic  1.6 us (2%)
    pallas_call x1, Pallas kernels, per_device(): pl.pallas_call(kernel, name='contrast', out_shape=(jax.ShapeDtypeStruct((...  63 us

profile of v6, /device:TPU:6, one launch (start us, length us, event | category | flops | bytes accessed | tf_op | source)
XLA Modules:
  0.0 65.8 jit_solution(18048569927027430469)
XLA Ops:
  0.6 0.7 %pad_add_fusion.meta_h = s32[4]{0:T(128)S(1)} fusion(s32[2]{0:T(128)} %param.8, s32[2]{0:T(128)} %param.7), kind=kLoop, calls=%fused_computation | loop fusion | flops 4 | bytes 32 | tf_op jit(solution)/shard_map/concatenate | solution.py:436
  1.4 63.0 %contrast.1 = (f32[8,128]{1,0:T(8,128)S(1)}, bf16[192,768]{1,0:T(8,128)(2,1)S(1)}) custom-call(s32[4]{0:T(128)S(1)} %pad_add_fusion.meta_h, bf16[640,768]{1,0:T(8,128)(2,1)} %tok_h.1, bf16[768,384]{1,0:T(8,128)(2,1)} %wq_h.1, bf16[768,768]{1,0:T(8,128)(2,1)} %wkv_h.1, bf16[384,768]{1,0:T(8,128)(2,1)} %wo_h.1), custom_call_target="tpu_custom_call" | custom-call | tf_op jit(solution)/shard_map/contrast/pallas_call | solution.py:393
  64.4 0.5 slice_bitcast_fusion
  64.9 0.9 %convert_element_type.3 = f32[192,768]{1,0:T(8,128)} convert(bf16[192,768]{1,0:T(8,128)(2,1)S(1)} %get-tuple-element.5) | non-fusion elementwise | flops 147456 | bytes 884736 | tf_op jit(solution)/shard_map/convert_element_type | solution.py:437

commit v7 on v6

--- a/solution.py
+++ b/solution.py
@@ -231,16 +231,11 @@
                     cp.start()
         for cp in fw:
             cp.wait_recv()
-        for cp in list(a2.values()) + a3 + fw:
-            cp.wait_send()
         for cp in e:
             cp.wait()
 
     pl.when(k == 0)(functools.partial(gather, 0))
     pl.when(k == 1)(functools.partial(gather, 1))
-    for cp in a1:
-        cp.wait_send()
-
     scale = 1.0 / SHARP
     whole = u[...].reshape(1024, 768)
     totals = [jnp.zeros((1, 256), F32)] * 4
@@ -316,6 +311,16 @@
         cp = remote(r2k_s.at[place[2]], r2k_r.at[j], r2k_ss.at[j], r2k_rs.at[j], place)
         cp.start()
         r2k.append(cp)
+    r3k, r3v, ag = [], [], []
+    sum2 = r2v_s[y].astype(F32)
+    for cp, j in zip(r2v, NEAR):
+        cp.wait_recv()
+        sum2 = sum2 + r2v_r[j].astype(F32)
+    r3v_r[z] = sum2.astype(BF)
+    for j in NEAR:
+        cp = remote(r3v_r.at[z], r3v_r.at[z], r3v_ss.at[j], r3v_rs.at[j], at(0, 0, j, 0))
+        cp.start()
+        r3v.append(cp)
     sum2 = r2k_s[z].astype(F32)
     for cp, j in zip(r2k, NEAR):
         cp.wait_recv()
@@ -324,7 +329,6 @@
         half = sum2[8 * i : 8 * i + 8]
         tiles = [half[:, :128], half[:, 128:256], half[:, 256:], jnp.zeros((8, 128), F32)]
         r3k_s[i] = jnp.concatenate(tiles, axis=0).astype(BF)
-    r3k, r3v = [], []
     for j in NEAR:
         place = at(0, j, 0, 0)
         src = r3k_s.at[lax.rem(place[1], 2)]
@@ -332,30 +336,7 @@
         cp.start()
         r3k.append(cp)
     r3k_r[y] = r3k_s[yl]
-    sum2 = r2v_s[y].astype(F32)
-    for cp, j in zip(r2v, NEAR):
-        cp.wait_recv()
-        sum2 = sum2 + r2v_r[j].astype(F32)
-    r3v_r[z] = sum2.astype(BF)
-    for j in NEAR:
-        cp = remote(r3v_r.at[z], r3v_r.at[z], r3v_ss.at[j], r3v_rs.at[j], at(0, 0, j, 0))
-        cp.start()
-        r3v.append(cp)
-
-    for cp in r3k:
-        cp.wait_recv()
-    sum3 = r3k_r[0].astype(F32)
-    for j in range(1, 8):
-        sum3 = sum3 + r3k_r[j].astype(F32)
-    mine = x * 8 + z
-    agk_r[mine] = sum3.astype(BF)
-    ag = []
-    for dx, dz in XZ:
-        slot = dx * 8 + dz
-        own = agk_r.at[mine]
-        cp = remote(own, own, agk_ss.at[slot], agk_rs.at[slot], at(dx, 0, dz, 0))
-        cp.start()
-        ag.append(cp)
+
     for cp in r3v:
         cp.wait_recv()
     sum3 = r3v_r[0].astype(F32)
@@ -367,6 +348,19 @@
         slot = dx * 4 + dh
         own = agv_r.at[mine_v]
         cp = remote(own, own, agv_ss.at[slot], agv_rs.at[slot], at(dx, 2 * dh, 0, 0))
+        cp.start()
+        ag.append(cp)
+    for cp in r3k:
+        cp.wait_recv()
+    sum3 = r3k_r[0].astype(F32)
+    for j in range(1, 8):
+        sum3 = sum3 + r3k_r[j].astype(F32)
+    mine = x * 8 + z
+    agk_r[mine] = sum3.astype(BF)
+    for dx, dz in XZ:
+        slot = dx * 8 + dz
+        own = agk_r.at[mine]
+        cp = remote(own, own, agk_ss.at[slot], agk_rs.at[slot], at(dx, 0, dz, 0))
         cp.start()
         ag.append(cp)
     krow = lax.broadcasted_iota(jnp.int32, (192, 1024), 0)
@@ -383,7 +377,13 @@
     for c in range(3):
         grad_out[:, 128 * c : 128 * c + 128] = mm(ksel[c], pieces).astype(BF)
     grad_out[:, 384:] = mm(vsel, agv_r[...].reshape(256, 384)).astype(BF)
-    for cp in dm + late + r2k + r2v + r3k + r3v + ag:
+    one, eight = u.at[0, 0, :, 0:384], u.at[0, :, :, 0:384]
+    for j in NEAR:
+        remote(one, one, a2_ss.at[j], a2_rs.at[j], at(0, j, 0, 0)).wait_send()
+        remote(eight, eight, a3_ss.at[j], a3_rs.at[j], at(0, j, 0, 0)).wait_send()
+    for j in range(8):
+        remote(eight, eight, fw_ss.at[j], fw_rs.at[j], at(0, 0, 0, 1)).wait_send()
+    for cp in a1 + dm + late + r2k + r2v + r3k + r3v + ag:
         cp.wait_send()
 
 

time: 66.5 us -> 65.5 us (0.985)
  no operation moved by 1% of the time
where the time goes in v7:
time: 65.5 us; the launch traced here: 65.3 us
  Pallas kernels  62.5 us (95%)
  other arithmetic  1.6 us (2%)
    pallas_call x1, Pallas kernels, per_device(): pl.pallas_call(kernel, name='contrast', out_shape=(jax.ShapeDtypeStruct((...  62.5 us

profile of v7, /device:TPU:6, one launch (start us, length us, event | category | flops | bytes accessed | tf_op | source)
XLA Modules:
  0.0 65.3 jit_solution(4316919431895060858)
XLA Ops:
  0.6 0.7 %pad_add_fusion.meta_h = s32[4]{0:T(128)S(1)} fusion(s32[2]{0:T(128)} %param.8, s32[2]{0:T(128)} %param.7), kind=kLoop, calls=%fused_computation | loop fusion | flops 4 | bytes 32 | tf_op jit(solution)/shard_map/concatenate | solution.py:436
  1.4 62.5 %contrast.1 = (f32[8,128]{1,0:T(8,128)S(1)}, bf16[192,768]{1,0:T(8,128)(2,1)S(1)}) custom-call(s32[4]{0:T(128)S(1)} %pad_add_fusion.meta_h, bf16[640,768]{1,0:T(8,128)(2,1)} %tok_h.1, bf16[768,384]{1,0:T(8,128)(2,1)} %wq_h.1, bf16[768,768]{1,0:T(8,128)(2,1)} %wkv_h.1, bf16[384,768]{1,0:T(8,128)(2,1)} %wo_h.1), custom_call_target="tpu_custom_call" | custom-call | tf_op jit(solution)/shard_map/contrast/pallas_call | solution.py:393
  63.9 0.5 slice_bitcast_fusion
  64.4 0.9 %convert_element_type.3 = f32[192,768]{1,0:T(8,128)} convert(bf16[192,768]{1,0:T(8,128)(2,1)S(1)} %get-tuple-element.5) | non-fusion elementwise | flops 147456 | bytes 884736 | tf_op jit(solution)/shard_map/convert_element_type | solution.py:437

commit v8 on v7

--- a/solution.py
+++ b/solution.py
@@ -94,13 +94,12 @@
             device_id=device(*place), device_id_type=MESH,
         )
 
-    loads = [
-        pltpu.make_async_copy(src, dst, in_s.at[i])
-        for i, (src, dst) in enumerate(
-            [(meta_h, meta), (tok_h, tok), (wq_h, wq), (wkv_h, wkv), (wo_h, wo)]
-        )
-    ]
-    for cp in loads:
+    parts = [(meta_h, meta)]
+    parts += [(tok_h.at[160 * i : 160 * i + 160], tok.at[160 * i : 160 * i + 160]) for i in range(4)]
+    parts += [(wq_h, wq), (wkv_h.at[:, 0:384], wkv.at[:, 0:384])]
+    parts += [(wkv_h.at[:, 384:768], wkv.at[:, 384:768]), (wo_h, wo)]
+    loads = [pltpu.make_async_copy(src, dst, in_s.at[i]) for i, (src, dst) in enumerate(parts)]
+    for cp in loads[:7]:
         cp.start()
     barrier = pltpu.get_barrier_semaphore()
     for off in PEERS:
@@ -110,8 +109,10 @@
 
     row = lax.broadcasted_iota(jnp.int32, (16, 640), 0)
     pos = lax.broadcasted_iota(jnp.int32, (16, 640), 1)
-    loads[0].wait()
-    loads[1].wait()
+    for cp in loads[:5]:
+        cp.wait()
+    for cp in loads[7:]:
+        cp.start()
     l0, l1 = meta[0], meta[1]
     lo = jnp.where(row < 8, 0, l0)
     hi = jnp.where(row < 8, l0, l0 + l1)
@@ -119,11 +120,11 @@
     first = mm((pos == lo).astype(F32).astype(BF), t)
     hrow = lax.rem(lax.broadcasted_iota(jnp.int32, (16, 384), 0), 8)
     own_head = lax.broadcasted_iota(jnp.int32, (16, 384), 1) // HEAD == hrow
-    loads[2].wait()
+    loads[5].wait()
     query = mm(first.astype(BF), wq[...]).astype(BF).astype(F32)
     qexp = jnp.where(own_head, query, 0.0).astype(BF)
-    loads[3].wait()
-    wk, wv = wkv[:, :384], wkv[:, 384:]
+    loads[6].wait()
+    wk = wkv[:, :384]
     scores = fold(mm_t(two(mm_t(qexp, wk)), t)) * HEAD ** (-0.5)
     scores = jnp.where((pos >= lo) & (pos < hi), scores, -1e30)
     lifted = jnp.exp(scores - jnp.max(scores, axis=1, keepdims=True))
@@ -132,10 +133,12 @@
     wb = weights.astype(BF)
     pooled = mm(wb, t)
     pooled_b = pooled.astype(BF)
+    loads[7].wait()
+    wv = wkv[:, 384:]
     mixed = jnp.where(own_head, fold(mm(two(pooled), wv)), 0.0)
     mixed = jnp.sum(mixed.reshape(2, 8, 384), axis=1, keepdims=True)
     mixed = jnp.broadcast_to(mixed, (2, 8, 384)).reshape(16, 384).astype(BF)
-    loads[4].wait()
+    loads[8].wait()
     embed = first + mm(mixed, wo[...])
     norm = jnp.sqrt(jnp.sum(embed * embed, axis=1, keepdims=True) + 1e-06)
     unit = embed / norm
@@ -405,7 +408,7 @@
             pltpu.VMEM((768, 384), BF),
             pltpu.VMEM((768, 768), BF),
             pltpu.VMEM((384, 768), BF),
-            dma((5,)),
+            dma((9,)),
             pltpu.VMEM((2, 16, 384), BF),
             pltpu.VMEM((8, 16, 384), BF),
             pltpu.VMEM((8, 8, 16, 768), BF),

time: 65.5 us -> 65.4 us (level)
  no operation moved by 1% of the time
where the time goes in v8:
time: 65.4 us; the launch traced here: 64.9 us
  Pallas kernels  62.1 us (95%)
  other arithmetic  1.6 us (2%)
    pallas_call x1, Pallas kernels, per_device(): pl.pallas_call(kernel, name='contrast', out_shape=(jax.ShapeDtypeStruct((...  62.1 us

profile of v8, /device:TPU:6, one launch (start us, length us, event | category | flops | bytes accessed | tf_op | source)
XLA Modules:
  0.0 64.9 jit_solution(6182194135991759738)
XLA Ops:
  0.6 0.7 %pad_add_fusion.meta_h = s32[4]{0:T(128)S(1)} fusion(s32[2]{0:T(128)} %param.8, s32[2]{0:T(128)} %param.7), kind=kLoop, calls=%fused_computation | loop fusion | flops 4 | bytes 32 | tf_op jit(solution)/shard_map/concatenate | solution.py:439
  1.4 62.1 %contrast.1 = (f32[8,128]{1,0:T(8,128)S(1)}, bf16[192,768]{1,0:T(8,128)(2,1)S(1)}) custom-call(s32[4]{0:T(128)S(1)} %pad_add_fusion.meta_h, bf16[640,768]{1,0:T(8,128)(2,1)} %tok_h.1, bf16[768,384]{1,0:T(8,128)(2,1)} %wq_h.1, bf16[768,768]{1,0:T(8,128)(2,1)} %wkv_h.1, bf16[384,768]{1,0:T(8,128)(2,1)} %wo_h.1), custom_call_target="tpu_custom_call" | custom-call | tf_op jit(solution)/shard_map/contrast/pallas_call | solution.py:396
  63.5 0.5 slice_bitcast_fusion
  64.0 0.9 %convert_element_type.3 = f32[192,768]{1,0:T(8,128)} convert(bf16[192,768]{1,0:T(8,128)(2,1)S(1)} %get-tuple-element.5) | non-fusion elementwise | flops 147456 | bytes 884736 | tf_op jit(solution)/shard_map/convert_element_type | solution.py:440
